TPU v7x, 32 devices: a whole 2x2x4 slice. The times are simulated.
32 devices in a mesh: occ: 4 (over x, core), vir: 8 (over z, y).
Axes of the slice: x: 2, y: 2, z: 4, core: 2. Of those that a mesh axis runs over, the one named last changes fastest.
Arguments:
- amplitudes: bfloat16 [4096, 256], P(('vir', 'occ')), may hold values from -6 to 6
- pair_irrep: int32 [32], P('vir'), may hold values from 0 to 7
- integrals: bfloat16 [8, 8, 128, 512], P('vir', None, None, 'occ'), may hold values from -0.375 to 0.375
- panel_blocks: int32 [8, 8], P('vir'), may hold values from 0 to 7, each once within a row
- panel_owner: int32 [2], replicated, may hold values from 0 to 7
Outputs:
- ladder: bfloat16 [4096, 512], P('vir', 'occ')
Inputs may be any that keep to these rules, and one draw needn't show every extreme that they name: Each row of panel_blocks names every irrep once.
All inputs are finite; a program needn't handle non-finite values.
Results may differ from a plain program's by a relative error of at most 0.001.
Values may be sent and summed in bfloat16 or wider, within the bound.
A program may use at most 64 MiB of HBM per device.

v0:
```python
import jax
import jax.numpy as jnp
from jax import lax
from jax.sharding import PartitionSpec as P


def from_root(block, axis, owner):
    block = jnp.where(lax.axis_index(axis) == owner, block, jnp.zeros_like(block))
    return lax.psum(block, axis)


def irrep_order(panel_data, blocks):
    irreps = blocks.shape[0]
    irrep_ids = jnp.arange(irreps, dtype=jnp.int32)
    matches = blocks[None, :] == irrep_ids[:, None]
    slot_ids = jnp.sum(jnp.where(matches, irrep_ids[None, :], 0), axis=1)
    return jnp.take(panel_data, slot_ids, axis=0)


def contract(amp_rows, labels, ordered, pair_dev):
    count_rows = amp_rows.shape[0]
    per_tile = min(count_rows, pair_dev)
    members = count_rows // per_tile
    row_width = amp_rows.shape[1]
    member_ids = jnp.arange(members, dtype=jnp.int32)
    matches = member_ids[:, None] == jnp.arange(labels.shape[0], dtype=jnp.int32)[None, :]
    irrep_ids = jnp.sum(jnp.where(matches, labels[None, :], 0), axis=1)
    group_size = max((option for option in (1, 2, 4) if members % option == 0))
    amp_tiles = amp_rows.reshape(members // group_size, group_size, per_tile, row_width)
    irrep_ids = irrep_ids.reshape(members // group_size, group_size)

    def contract_turn(state_carry, inputs):
        tile_block, chosen = inputs
        weights = jnp.concatenate(
            [jnp.take(one_panel, chosen, axis=0) for one_panel in ordered], axis=1
        )
        result = jnp.einsum("gpk,gkc->gpc", tile_block, weights, preferred_element_type=jnp.float32)
        return (state_carry, result.astype(jnp.bfloat16))

    unused, outputs = lax.scan(contract_turn, jnp.int32(0), (amp_tiles, irrep_ids))
    return outputs.reshape(count_rows, outputs.shape[-1])


def per_device(amplitudes, pair_irrep, integrals, panel_blocks, panel_owner):
    pair_dev = amplitudes.shape[0]
    own_panel = irrep_order(integrals[0], panel_blocks[0])
    ordered = []
    for step_index in range(panel_owner.shape[0]):
        ordered.append(from_root(own_panel, "vir", panel_owner[step_index]))
    gathered = lax.all_gather(amplitudes, "occ", axis=0, tiled=True)
    return contract(gathered, pair_irrep, ordered, pair_dev)


def solution(mesh):
    return jax.shard_map(
        per_device,
        mesh=mesh,
        in_specs=(
            P(("vir", "occ"), None),
            P("vir"),
            P("vir", None, None, "occ"),
            P("vir", None),
            P(),
        ),
        out_specs=P("vir", "occ"),
        check_vma=False,
    )
```

profile of v0, /device:TPU:0, one launch (start us, length us, event | category | flops | bytes accessed | tf_op | source)
XLA Modules:
  0.0 96.8 jit_solution(487444578109391582)
XLA Ops:
  6.5 0.0 copy-start
  6.5 0.0 all-reduce.3.cloned.1.call-start
  6.5 0.0 copy-start.4
  6.5 0.7 copy-done.4
  7.2 0.1 select_reduce_fusion
  7.4 0.0 copy-start.3
  7.4 0.6 copy-done.3
  8.0 0.6 fusion.5
  9.8 0.0 copy-done
  9.8 0.6 gather_fusion
  10.4 0.9 broadcast_select_fusion.2
  11.4 0.0 copy-start.5
  11.4 0.0 copy-start.1
  11.4 0.0 all-reduce.3.cloned.1.call-update
  11.4 0.6 copy-done.5
  12.0 0.1 select_reduce_fusion.1
  12.1 0.1 copy-done.1
  12.2 7.2 %all_gather.3 = bf16[512,256]{1,0:T(8,128)(2,1)S(1)} all-gather(bf16[128,256]{1,0:T(8,128)(2,1)S(1)} %copy-done.1), channel_id=1, replica_groups=mesh['occ'=4,'vir'=8] {'occ'}, dimensions={0}, use_global_device_ids=true | all-gather | bytes 327680 | tf_op jit(solution)/shard_map/all_gather | solution.py:50
  19.4 67.4 %all-reduce.3.cloned.1.call-done = (bf16[8,128,128]{2,1,0:T(8,128)(2,1)}, bf16[8,128,128]{2,1,0:T(8,128)(2,1)}) async-done(((bf16[8,128,128]{2,1,0:T(8,128)(2,1)}, bf16[8,128,128]{2,1,0:T(8,128)(2,1)}), (bf16[8,128,128]{2,1,0:T(8,128)(2,1)}, bf16[8,128,128]{2,1,0:T(8,128)(2,1)})) %all-reduce.3.cloned.1.call-update) | async-done | bytes 524304 | tf_op jit(solution)/shard_map/psum | solution.py:9
  86.8 1.6 %gather_fusion.1 = bf16[4,128,128]{2,1,0:T(8,128)(2,1)S(1)} fusion(bf16[8,128,128]{2,1,0:T(8,128)(2,1)} %get-tuple-element.17, s32[1024]{0:T(1024)S(1)} %pad_clamp_fusion), kind=kCustom, calls=%fused_computation.clone | custom fusion | bytes 262160 | tf_op jit(solution)/shard_map/while/body/eval_jaxpr/jit(_take)/gather | solution.py:35
  88.4 0.0 copy-done.2
  88.4 0.6 gather_fusion.2
  88.9 0.1 broadcast_select_fusion.4
  89.0 0.9 convolution_convert_fusion
  (7 shorter events, 0.0 us)
Async XLA Ops:
  6.5 3.3 %copy-start = (bf16[1,8,128,128]{3,2,1,0:T(8,128)(2,1)S(1)}, bf16[1,8,128,128]{3,2,1,0:T(8,128)(2,1)}, u32[]{:S(2)}) copy-start(bf16[1,8,128,128]{3,2,1,0:T(8,128)(2,1)} %param.9) | copy-start | bytes 786436
  6.5 80.2 %all-reduce.3.cloned.1.call-start = ((), (), s32[]{:S(2)}) async-start(), calls=%async_computation | async-start | bytes 1048576 | tf_op jit(solution)/shard_map/psum | solution.py:9
  6.5 0.7 copy-start.4
  7.4 0.7 copy-start.3
  11.4 0.7 copy-start.5
  11.4 0.9 copy-start.1
  86.8 1.6 %copy-start.2 = (bf16[8,128,128]{2,1,0:T(8,128)(2,1)S(1)}, bf16[8,128,128]{2,1,0:T(8,128)(2,1)}, u32[]{:S(2)}) copy-start(bf16[8,128,128]{2,1,0:T(8,128)(2,1)} %get-tuple-element.16) | copy-start | bytes 786436
Sparse Core Ops, SparseCore 0:
  11.5 75.2 all-reduce.2
where the time goes:
time: 97 us; the launch traced here: 96.8 us
  waiting for transfers between devices  67.4 us (69%)
  between operations  14.7 us (15%)
  blocking collectives  7.18 us (7%)
  local copies, waits for them, and re-layouts  5.38 us (6%)
  other arithmetic  1.28 us (1%)
    psum x1, waiting for transfers between devices, from_root(): return lax.psum(block, axis)  67.4 us
    all_gather x1, blocking collectives, per_device(): gathered = lax.all_gather(amplitudes, 'occ', axis=0, tiled=True)  7.18 us
    gather x2, local copies, waits for them, and re-layouts, contract_turn(): jnp.take(one_panel, chosen, axis=0)  2.14 us
    unnamed x12, local copies, waits for them, and re-layouts  2.07 us
  transfers between devices with their start and end apart: 1, of which 1 were waited for; matrix products, arithmetic and copies ran while one was open for 0% of the time, Pallas kernels for 0%

commit v1 on v0

v1 whole, which is shorter than its diff:
```python
import functools

import jax
import jax.numpy as jnp
from jax import lax
from jax.experimental import pallas as pl
from jax.experimental.pallas import tpu as pltpu
from jax.sharding import PartitionSpec as P

MESH = pl.DeviceIdType.MESH
ROWS = 16


def guarded(always, condition, run):
    if always:
        run()
    else:
        pl.when(condition)(run)


def ladder_kernel(
    n_vir, n_occ, relays, by_tile,
    labels_ref, blocks_ref, owner_ref, amp_ref, panel_ref, out_ref,
    info, info_all, info_smem, stage, got, picked, weights, amp_all,
    info_send, info_recv, one_send, one_recv, two_send, two_recv, amp_send, amp_recv, local_sem,
):
    vir, occ = lax.axis_index("vir"), lax.axis_index("occ")
    irreps = panel_ref.shape[0]
    steps = owner_ref.shape[0]
    tiles = labels_ref.shape[0]
    piece = stage.shape[2]
    pair_dev = amp_ref.shape[0]
    full = relays == n_vir
    is_relay = vir < relays

    barrier = pltpu.get_barrier_semaphore()
    for d in range(1, n_vir):
        pl.semaphore_signal(barrier, inc=1, device_id={"vir": lax.rem(vir + d, n_vir)}, device_id_type=MESH)
    for d in range(1, n_occ):
        pl.semaphore_signal(barrier, inc=1, device_id={"occ": lax.rem(occ + d, n_occ)}, device_id_type=MESH)

    lanes = lax.broadcasted_iota(jnp.int32, info.shape, 1)
    row = jnp.zeros(info.shape, jnp.int32)
    for t in range(tiles):
        row = jnp.where(lanes == t, labels_ref[t], row)
    info[...] = row
    info_all[vir] = row
    for g in range(irreps):
        slot = jnp.int32(0)
        for b in range(irreps):
            slot = jnp.where(blocks_ref[0, b] == g, b, slot)
        block = panel_ref[slot]
        for w in range(relays):
            stage[w, g] = block[w * piece:(w + 1) * piece]

    pl.semaphore_wait(barrier, n_vir - 1 + n_occ - 1)

    def info_copy(d):
        return pltpu.make_async_remote_copy(
            src_ref=info, dst_ref=info_all.at[vir], send_sem=info_send.at[d], recv_sem=info_recv.at[d],
            device_id={"vir": lax.rem(vir + d, n_vir)}, device_id_type=MESH)

    def one_copy(d):
        to = lax.rem(vir + d, n_vir)
        return pltpu.make_async_remote_copy(
            src_ref=stage.at[to], dst_ref=got.at[vir], send_sem=one_send.at[d], recv_sem=one_recv.at[d],
            device_id={"vir": to}, device_id_type=MESH)

    def two_copy(d):
        return pltpu.make_async_remote_copy(
            src_ref=picked.at[d if by_tile else 0],
            dst_ref=weights.at[:, :, pl.ds(pl.multiple_of(vir * piece, piece), piece), :],
            send_sem=two_send.at[d], recv_sem=two_recv.at[d],
            device_id={"vir": lax.rem(vir + d, n_vir)}, device_id_type=MESH)

    def amp_copy(d):
        return pltpu.make_async_remote_copy(
            src_ref=amp_ref, dst_ref=amp_all.at[occ], send_sem=amp_send.at[d], recv_sem=amp_recv.at[d],
            device_id={"occ": lax.rem(occ + d, n_occ)}, device_id_type=MESH)

    def wait_one_from_stage(d):
        pltpu.make_async_remote_copy(
            src_ref=stage.at[0], dst_ref=got.at[vir], send_sem=one_send.at[d], recv_sem=one_recv.at[d],
            device_id={"vir": lax.rem(vir + d, n_vir)}, device_id_type=MESH).wait_recv()

    if by_tile:
        for d in range(1, n_vir):
            guarded(full, lax.rem(vir + d, n_vir) < relays, lambda d=d: info_copy(d).start())
    for d in range(1, n_vir):
        guarded(full, lax.rem(vir + d, n_vir) < relays, lambda d=d: one_copy(d).start())
    for d in range(1, n_occ):
        amp_copy(d).start()

    amp_all[occ] = amp_ref[...]

    def relay():
        got[vir] = stage[vir]
        if by_tile:
            for d in range(1, n_vir):
                info_copy(d).wait_recv()
            to_smem = pltpu.make_async_copy(info_all, info_smem, local_sem)
            to_smem.start()
            to_smem.wait()
        for d in range(1, n_vir):
            wait_one_from_stage(d)
        owners = [owner_ref[s] for s in range(steps)]
        for d in list(range(1, n_vir)) + [0]:
            to = lax.rem(vir + d, n_vir)
            if by_tile:
                for t in range(tiles):
                    irrep = info_smem[to, 0, t]
                    for s in range(steps):
                        picked[d, t, s] = got[owners[s], irrep]
            elif d == 1 or n_vir == 1:
                for g in range(irreps):
                    for s in range(steps):
                        picked[0, g, s] = got[owners[s], g]
            if d:
                two_copy(d).start()
        weights[:, :, pl.ds(pl.multiple_of(vir * piece, piece), piece), :] = picked[0]

    guarded(full, is_relay, relay)

    for d in range(1, n_occ):
        amp_copy(d).wait_recv()
    for d in range(1, n_vir):
        guarded(full, lax.rem(vir + n_vir - d, n_vir) < relays, lambda d=d: two_copy(d).wait_recv())

    def tile(t):
        chosen = weights[t if by_tile else labels_ref[t]]
        chosen = chosen.reshape(chosen.shape[0] * chosen.shape[1], chosen.shape[2])
        result = jnp.dot(amp_all[t], chosen, preferred_element_type=jnp.float32)
        out_ref[pl.ds(pl.multiple_of(t * pair_dev, pair_dev), pair_dev), :] = result.astype(out_ref.dtype)

    if tiles <= 8:
        for t in range(tiles):
            tile(t)
    else:
        pl.loop(0, tiles)(tile)

    for d in range(1, n_occ):
        amp_copy(d).wait_send()
    for d in range(1, n_vir):
        if by_tile:
            guarded(full, lax.rem(vir + d, n_vir) < relays, lambda d=d: info_copy(d).wait_send())
        guarded(full, lax.rem(vir + d, n_vir) < relays, lambda d=d: one_copy(d).wait_send())
        guarded(full, is_relay, lambda d=d: two_copy(d).wait_send())


def per_device(n_vir, n_occ, amplitudes, pair_irrep, integrals, panel_blocks, panel_owner):
    pair_dev, width = amplitudes.shape
    _, irreps, depth, columns = integrals.shape
    tiles = pair_irrep.shape[0]
    steps = panel_owner.shape[0]
    relays = min(n_vir, depth // ROWS)
    piece = depth // relays
    by_tile = tiles < irreps
    choices = min(tiles, irreps)
    lanes = -(-tiles // 128) * 128
    kind = amplitudes.dtype
    smem = pl.BlockSpec(memory_space=pltpu.SMEM)
    vmem = pl.BlockSpec(memory_space=pltpu.VMEM)
    dma = pltpu.SemaphoreType.DMA
    return pl.pallas_call(
        functools.partial(ladder_kernel, n_vir, n_occ, relays, by_tile),
        out_shape=jax.ShapeDtypeStruct((tiles * pair_dev, columns), kind),
        in_specs=[smem, smem, smem, vmem, vmem],
        out_specs=vmem,
        scratch_shapes=[
            pltpu.VMEM((1, lanes), jnp.int32),
            pltpu.VMEM((n_vir, 1, lanes), jnp.int32),
            pltpu.SMEM((n_vir, 1, lanes), jnp.int32),
            pltpu.VMEM((relays, irreps, piece, columns), kind),
            pltpu.VMEM((n_vir, irreps, piece, columns), kind),
            pltpu.VMEM((n_vir if by_tile else 1, choices, steps, piece, columns), kind),
            pltpu.VMEM((choices, steps, depth, columns), kind),
            pltpu.VMEM((tiles, pair_dev, width), kind),
            dma((n_vir,)), dma((n_vir,)), dma((n_vir,)), dma((n_vir,)),
            dma((n_vir,)), dma((n_vir,)), dma((n_occ,)), dma((n_occ,)), dma,
        ],
        compiler_params=pltpu.CompilerParams(
            collective_id=0, has_side_effects=True, vmem_limit_bytes=32 * 1024 * 1024),
    )(pair_irrep, panel_blocks, panel_owner, amplitudes, integrals[0])


def solution(mesh):
    return jax.shard_map(
        functools.partial(per_device, mesh.shape["vir"], mesh.shape["occ"]),
        mesh=mesh,
        in_specs=(
            P(("vir", "occ"), None),
            P("vir"),
            P("vir", None, None, "occ"),
            P("vir", None),
            P(),
        ),
        out_specs=P("vir", "occ"),
        check_vma=False,
    )
```

time: 97 us -> 22.7 us (0.23)
  waiting for transfers between devices: 67.4 us -> 0 us
  Pallas kernels: 0 us -> 19.3 us
  between operations: 14.7 us -> 0.01 us
  blocking collectives: 7.18 us -> 0 us
  local copies, waits for them, and re-layouts: 5.38 us -> 3.13 us
  other arithmetic: 1.28 us -> 0 us
    psum x1 -> x0, waiting for transfers between devices: 67.4 us -> none  [from_root(): return lax.psum(block, axis)]
    pallas_call x0 -> x1, Pallas kernels: none -> 19.3 us  [per_device(): pl.pallas_call(functools.partial(ladder_kernel, n_vir, n_occ, relays, by_...]
    all_gather x1 -> x0, blocking collectives: 7.18 us -> none  [per_device(): gathered = lax.all_gather(amplitudes, 'occ', axis=0, tiled=True)]
    gather x3 -> x0, local copies, waits for them, and re-layouts: 2.73 us -> none  [the longest x2 2.14 us: contract_turn(): jnp.take(one_panel, chosen, axis=0)]
    unnamed x12 -> x11, local copies, waits for them, and re-layouts: 2.07 us -> 3.13 us
    select_n x4 -> x0, other arithmetic: 1.02 us -> none  [the longest x1 0.91 us: from_root(): jnp.where(lax.axis_index(axis) == owner, block, jnp.zeros_like(block))]
  transfers between devices with their start and end apart: 1 -> 0, of which waited for: 1 -> 0; matrix products, arithmetic and copies ran while one was open for 0% -> 0% of each run, Pallas kernels for 0% -> 0%
where the time goes in v1:
time: 22.7 us; the launch traced here: 22.5 us
  Pallas kernels  19.3 us (85%)
  local copies, waits for them, and re-layouts  3.13 us (14%)
    pallas_call x1, Pallas kernels, per_device(): pl.pallas_call(functools.partial(ladder_kernel, n_vir, n_occ, relays, by_...  19.3 us
    unnamed x11, local copies, waits for them, and re-layouts  3.13 us

profile of v1, /device:TPU:0, one launch (start us, length us, event | category | flops | bytes accessed | tf_op | source)
XLA Modules:
  0.0 22.5 jit_solution(11392236754967060060)
XLA Ops:
  0.0 0.0 copy-start.4
  0.0 0.0 copy-start.3
  0.0 0.0 copy-start.2
  0.0 0.6 %copy-done.4 = s32[2]{0:T(128)S(1)} copy-done((s32[2]{0:T(128)S(1)}, s32[2]{0:T(128)}, u32[]{:S(2)}) %copy-start.4) | copy-done | bytes 32
  0.7 0.0 copy-done.3
  0.7 0.0 copy-done.2
  0.7 0.0 copy-start
  0.7 0.9 %copy-done = bf16[1,8,128,128]{3,2,1,0:T(8,128)(2,1)S(1)} copy-done((bf16[1,8,128,128]{3,2,1,0:T(8,128)(2,1)S(1)}, bf16[1,8,128,128]{3,2,1,0:T(8,128)(2,1)}, u32[]{:S(2)}) %copy-start) | copy-done | bytes 262168
  1.6 0.0 copy-start.1
  1.6 0.8 %copy-done.1 = bf16[128,256]{1,0:T(8,128)(2,1)S(1)} copy-done((bf16[128,256]{1,0:T(8,128)(2,1)S(1)}, bf16[128,256]{1,0:T(8,128)(2,1)}, u32[]{:S(2)}) %copy-start.1) | copy-done | bytes 65560
  2.5 19.3 %shard_map.55 = bf16[512,128]{1,0:T(8,128)(2,1)S(1)} custom-call(s32[4]{0:T(128)S(1)} %copy-done.2, s32[1,8]{1,0:T(1,128)S(1)} %copy-done.3, s32[2]{0:T(128)S(1)} %copy-done.4, bf16[128,256]{1,0:T(8,128)(2,1)S(1)} %copy-done.1, bf16[8,128,128]{2,1,0:T(8,128)(2,1)S(1)} %bitcast.1), custom_call_target="tpu_custom_call" | custom-call | tf_op jit(solution)/shard_map/pallas_call | solution.py:164
  21.8 0.7 %copy.7 = bf16[512,128]{1,0:T(8,128)(2,1)} copy(bf16[512,128]{1,0:T(8,128)(2,1)S(1)} %shard_map.55) | data formatting | bytes 262144
Async XLA Ops:
  0.0 0.7 %copy-start.4 = (s32[2]{0:T(128)S(1)}, s32[2]{0:T(128)}, u32[]{:S(2)}) copy-start(s32[2]{0:T(128)} %owner_ref.1) | copy-start | bytes 28
  0.0 0.7 %copy-start.3 = (s32[1,8]{1,0:T(1,128)S(1)}, s32[1,8]{1,0:T(1,128)}, u32[]{:S(2)}) copy-start(s32[1,8]{1,0:T(1,128)} %blocks_ref.1) | copy-start | bytes 100
  0.0 0.7 %copy-start.2 = (s32[4]{0:T(128)S(1)}, s32[4]{0:T(128)}, u32[]{:S(2)}) copy-start(s32[4]{0:T(128)} %labels_ref.1) | copy-start | bytes 52
  0.7 0.9 %copy-start = (bf16[1,8,128,128]{3,2,1,0:T(8,128)(2,1)S(1)}, bf16[1,8,128,128]{3,2,1,0:T(8,128)(2,1)}, u32[]{:S(2)}) copy-start(bf16[1,8,128,128]{3,2,1,0:T(8,128)(2,1)} %param.7) | copy-start | bytes 786436
  1.6 0.8 %copy-start.1 = (bf16[128,256]{1,0:T(8,128)(2,1)S(1)}, bf16[128,256]{1,0:T(8,128)(2,1)}, u32[]{:S(2)}) copy-start(bf16[128,256]{1,0:T(8,128)(2,1)} %amp_ref.1) | copy-start | bytes 196612

commit v2 on v1

--- a/solution.py
+++ b/solution.py
@@ -20,9 +20,10 @@
 
 def ladder_kernel(
     n_vir, n_occ, relays, by_tile,
-    labels_ref, blocks_ref, owner_ref, amp_ref, panel_ref, out_ref,
+    labels_hbm, blocks_hbm, owner_hbm, amp_ref, panel_hbm, out_ref,
+    labels_ref, blocks_ref, owner_ref, panel_ref,
     info, info_all, info_smem, stage, got, picked, weights, amp_all,
-    info_send, info_recv, one_send, one_recv, two_send, two_recv, amp_send, amp_recv, local_sem,
+    info_send, info_recv, one_send, one_recv, two_send, two_recv, amp_send, amp_recv, local_sem, fetch_sem,
 ):
     vir, occ = lax.axis_index("vir"), lax.axis_index("occ")
     irreps = panel_ref.shape[0]
@@ -38,6 +39,18 @@
         pl.semaphore_signal(barrier, inc=1, device_id={"vir": lax.rem(vir + d, n_vir)}, device_id_type=MESH)
     for d in range(1, n_occ):
         pl.semaphore_signal(barrier, inc=1, device_id={"occ": lax.rem(occ + d, n_occ)}, device_id_type=MESH)
+
+    fetches = [
+        pltpu.make_async_copy(labels_hbm, labels_ref, fetch_sem.at[0]),
+        pltpu.make_async_copy(blocks_hbm, blocks_ref, fetch_sem.at[1]),
+        pltpu.make_async_copy(owner_hbm, owner_ref, fetch_sem.at[2]),
+        pltpu.make_async_copy(panel_hbm.at[0], panel_ref, fetch_sem.at[3]),
+        pltpu.make_async_copy(amp_ref, amp_all.at[occ], fetch_sem.at[4]),
+    ]
+    for fetch in fetches:
+        fetch.start()
+    for fetch in fetches:
+        fetch.wait()
 
     lanes = lax.broadcasted_iota(jnp.int32, info.shape, 1)
     row = jnp.zeros(info.shape, jnp.int32)
@@ -90,8 +103,6 @@
         guarded(full, lax.rem(vir + d, n_vir) < relays, lambda d=d: one_copy(d).start())
     for d in range(1, n_occ):
         amp_copy(d).start()
-
-    amp_all[occ] = amp_ref[...]
 
     def relay():
         got[vir] = stage[vir]
@@ -158,15 +169,18 @@
     choices = min(tiles, irreps)
     lanes = -(-tiles // 128) * 128
     kind = amplitudes.dtype
-    smem = pl.BlockSpec(memory_space=pltpu.SMEM)
-    vmem = pl.BlockSpec(memory_space=pltpu.VMEM)
+    hbm = pl.BlockSpec(memory_space=pltpu.HBM)
     dma = pltpu.SemaphoreType.DMA
     return pl.pallas_call(
         functools.partial(ladder_kernel, n_vir, n_occ, relays, by_tile),
         out_shape=jax.ShapeDtypeStruct((tiles * pair_dev, columns), kind),
-        in_specs=[smem, smem, smem, vmem, vmem],
-        out_specs=vmem,
+        in_specs=[hbm] * 5,
+        out_specs=pl.BlockSpec(memory_space=pltpu.VMEM),
         scratch_shapes=[
+            pltpu.SMEM(pair_irrep.shape, jnp.int32),
+            pltpu.SMEM(panel_blocks.shape, jnp.int32),
+            pltpu.SMEM(panel_owner.shape, jnp.int32),
+            pltpu.VMEM(integrals.shape[1:], kind),
             pltpu.VMEM((1, lanes), jnp.int32),
             pltpu.VMEM((n_vir, 1, lanes), jnp.int32),
             pltpu.SMEM((n_vir, 1, lanes), jnp.int32),
@@ -176,11 +190,11 @@
             pltpu.VMEM((choices, steps, depth, columns), kind),
             pltpu.VMEM((tiles, pair_dev, width), kind),
             dma((n_vir,)), dma((n_vir,)), dma((n_vir,)), dma((n_vir,)),
-            dma((n_vir,)), dma((n_vir,)), dma((n_occ,)), dma((n_occ,)), dma,
+            dma((n_vir,)), dma((n_vir,)), dma((n_occ,)), dma((n_occ,)), dma, dma((5,)),
         ],
         compiler_params=pltpu.CompilerParams(
-            collective_id=0, has_side_effects=True, vmem_limit_bytes=32 * 1024 * 1024),
-    )(pair_irrep, panel_blocks, panel_owner, amplitudes, integrals[0])
+            collective_id=0, has_side_effects=True, vmem_limit_bytes=60 * 1024 * 1024),
+    )(pair_irrep, panel_blocks, panel_owner, amplitudes, integrals)
 
 
 def solution(mesh):

time: 22.7 us -> 21.2 us (0.934)
  local copies, waits for them, and re-layouts: 3.13 us -> 1.57 us
    unnamed x11 -> x1, local copies, waits for them, and re-layouts: 3.13 us -> 1.57 us
where the time goes in v2:
time: 21.2 us; the launch traced here: 21 us
  Pallas kernels  19.4 us (92%)
  local copies, waits for them, and re-layouts  1.57 us (7%)
    pallas_call x1, Pallas kernels, per_device(): pl.pallas_call(functools.partial(ladder_kernel, n_vir, n_occ, relays, by_...  19.4 us
    unnamed x1, local copies, waits for them, and re-layouts  1.57 us

profile of v2, /device:TPU:0, one launch (start us, length us, event | category | flops | bytes accessed | tf_op | source)
XLA Modules:
  0.0 21.0 jit_solution(8710603162483469134)
XLA Ops:
  0.0 19.4 %shard_map.55 = bf16[512,128]{1,0:T(8,128)(2,1)} custom-call(s32[4]{0:T(128)} %labels_hbm.1, s32[1,8]{1,0:T(1,128)} %blocks_hbm.1, s32[2]{0:T(128)} %owner_hbm.1, bf16[128,256]{1,0:T(8,128)(2,1)} %amp_ref.1, bf16[1,8,128,128]{3,2,1,0:T(8,128)(2,1)} %panel_hbm.1), custom_call_target="tpu_custom_call" | custom-call | tf_op jit(solution)/shard_map/pallas_call | solution.py:174
  19.4 1.6 %copy.7 = bf16[512,128]{1,0:T(8,128)(2,1)} copy(bf16[512,128]{1,0:T(8,128)(2,1)} %shard_map.55) | data formatting | bytes 262144

commit v3 on v2

--- a/solution.py
+++ b/solution.py
@@ -20,9 +20,9 @@
 
 def ladder_kernel(
     n_vir, n_occ, relays, by_tile,
-    labels_hbm, blocks_hbm, owner_hbm, amp_ref, panel_hbm, out_ref,
+    labels_hbm, blocks_hbm, owner_hbm, amp_ref, panel_hbm, amp_all, weights,
     labels_ref, blocks_ref, owner_ref, panel_ref,
-    info, info_all, info_smem, stage, got, picked, weights, amp_all,
+    info, info_all, info_smem, stage, got, picked,
     info_send, info_recv, one_send, one_recv, two_send, two_recv, amp_send, amp_recv, local_sem, fetch_sem,
 ):
     vir, occ = lax.axis_index("vir"), lax.axis_index("occ")
@@ -30,7 +30,6 @@
     steps = owner_ref.shape[0]
     tiles = labels_ref.shape[0]
     piece = stage.shape[2]
-    pair_dev = amp_ref.shape[0]
     full = relays == n_vir
     is_relay = vir < relays
 
@@ -49,7 +48,7 @@
     ]
     for fetch in fetches:
         fetch.start()
-    for fetch in fetches:
+    for fetch in fetches[:4]:
         fetch.wait()
 
     lanes = lax.broadcasted_iota(jnp.int32, info.shape, 1)
@@ -85,6 +84,10 @@
             dst_ref=weights.at[:, :, pl.ds(pl.multiple_of(vir * piece, piece), piece), :],
             send_sem=two_send.at[d], recv_sem=two_recv.at[d],
             device_id={"vir": lax.rem(vir + d, n_vir)}, device_id_type=MESH)
+
+    def own_rows():
+        return pltpu.make_async_copy(
+            picked.at[0], weights.at[:, :, pl.ds(pl.multiple_of(vir * piece, piece), piece), :], local_sem)
 
     def amp_copy(d):
         return pltpu.make_async_remote_copy(
@@ -128,7 +131,7 @@
                         picked[0, g, s] = got[owners[s], g]
             if d:
                 two_copy(d).start()
-        weights[:, :, pl.ds(pl.multiple_of(vir * piece, piece), piece), :] = picked[0]
+        own_rows().start()
 
     guarded(full, is_relay, relay)
 
@@ -137,18 +140,8 @@
     for d in range(1, n_vir):
         guarded(full, lax.rem(vir + n_vir - d, n_vir) < relays, lambda d=d: two_copy(d).wait_recv())
 
-    def tile(t):
-        chosen = weights[t if by_tile else labels_ref[t]]
-        chosen = chosen.reshape(chosen.shape[0] * chosen.shape[1], chosen.shape[2])
-        result = jnp.dot(amp_all[t], chosen, preferred_element_type=jnp.float32)
-        out_ref[pl.ds(pl.multiple_of(t * pair_dev, pair_dev), pair_dev), :] = result.astype(out_ref.dtype)
-
-    if tiles <= 8:
-        for t in range(tiles):
-            tile(t)
-    else:
-        pl.loop(0, tiles)(tile)
-
+    fetches[4].wait()
+    guarded(full, is_relay, lambda: own_rows().wait())
     for d in range(1, n_occ):
         amp_copy(d).wait_send()
     for d in range(1, n_vir):
@@ -171,11 +164,14 @@
     kind = amplitudes.dtype
     hbm = pl.BlockSpec(memory_space=pltpu.HBM)
     dma = pltpu.SemaphoreType.DMA
-    return pl.pallas_call(
+    gathered, weights = pl.pallas_call(
         functools.partial(ladder_kernel, n_vir, n_occ, relays, by_tile),
-        out_shape=jax.ShapeDtypeStruct((tiles * pair_dev, columns), kind),
+        out_shape=(
+            jax.ShapeDtypeStruct((tiles, pair_dev, width), kind),
+            jax.ShapeDtypeStruct((choices, steps, depth, columns), kind),
+        ),
         in_specs=[hbm] * 5,
-        out_specs=pl.BlockSpec(memory_space=pltpu.VMEM),
+        out_specs=(hbm, hbm),
         scratch_shapes=[
             pltpu.SMEM(pair_irrep.shape, jnp.int32),
             pltpu.SMEM(panel_blocks.shape, jnp.int32),
@@ -187,14 +183,23 @@
             pltpu.VMEM((relays, irreps, piece, columns), kind),
             pltpu.VMEM((n_vir, irreps, piece, columns), kind),
             pltpu.VMEM((n_vir if by_tile else 1, choices, steps, piece, columns), kind),
-            pltpu.VMEM((choices, steps, depth, columns), kind),
-            pltpu.VMEM((tiles, pair_dev, width), kind),
             dma((n_vir,)), dma((n_vir,)), dma((n_vir,)), dma((n_vir,)),
             dma((n_vir,)), dma((n_vir,)), dma((n_occ,)), dma((n_occ,)), dma, dma((5,)),
         ],
         compiler_params=pltpu.CompilerParams(
             collective_id=0, has_side_effects=True, vmem_limit_bytes=60 * 1024 * 1024),
     )(pair_irrep, panel_blocks, panel_owner, amplitudes, integrals)
+    weights = weights.reshape(choices, steps * depth, columns)
+    if by_tile:
+        result = jnp.einsum("tpk,tkc->tpc", gathered, weights, preferred_element_type=jnp.float32)
+        return result.astype(kind).reshape(tiles * pair_dev, columns)
+
+    def tile_ladder(inputs):
+        rows, irrep = inputs
+        chosen = lax.dynamic_index_in_dim(weights, irrep, 0, keepdims=False)
+        return jnp.dot(rows, chosen, preferred_element_type=jnp.float32).astype(kind)
+
+    return lax.map(tile_ladder, (gathered, pair_irrep)).reshape(tiles * pair_dev, columns)
 
 
 def solution(mesh):

time: 21.2 us -> 20.7 us (0.976)
  matrix products: 0 us -> 1.9 us
  local copies, waits for them, and re-layouts: 1.57 us -> 0 us
  Pallas kernels: 19.4 us -> 18.7 us
    dot_general x0 -> x1, matrix products: none -> 1.9 us  [per_device(): jnp.einsum('tpk,tkc->tpc', gathered, weights, preferred_element_type=jnp....]
    unnamed x1 -> x0, local copies, waits for them, and re-layouts: 1.57 us -> none
    pallas_call x1, Pallas kernels: 19.4 us -> 18.7 us  [per_device(): pl.pallas_call(functools.partial(ladder_kernel, n_vir, n_occ, relays, by_...]
where the time goes in v3:
time: 20.7 us; the launch traced here: 20.6 us
  Pallas kernels  18.7 us (90%)
  matrix products  1.9 us (9%)
    pallas_call x1, Pallas kernels, per_device(): pl.pallas_call(functools.partial(ladder_kernel, n_vir, n_occ, relays, by_...  18.7 us
    dot_general x1, matrix products, per_device(): jnp.einsum('tpk,tkc->tpc', gathered, weights, preferred_element_type=jnp....  1.9 us

profile of v3, /device:TPU:0, one launch (start us, length us, event | category | flops | bytes accessed | tf_op | source)
XLA Modules:
  0.0 20.6 jit_solution(10287980078157818513)
XLA Ops:
  0.0 18.7 %shard_map.55 = (bf16[4,128,256]{2,1,0:T(8,128)(2,1)}, bf16[4,2,128,128]{3,2,1,0:T(8,128)(2,1)}) custom-call(s32[4]{0:T(128)} %labels_hbm.1, s32[1,8]{1,0:T(1,128)} %blocks_hbm.1, s32[2]{0:T(128)} %owner_hbm.1, bf16[128,256]{1,0:T(8,128)(2,1)} %amp_ref.1, bf16[1,8,128,128]{3,2,1,0:T(8,128)(2,1)} %panel_hbm.1), custom_call_target="tpu_custom_call" | custom-call | tf_op jit(solution)/shard_map/pallas_call | solution.py:167
  18.7 1.9 %convolution_convert_fusion = bf16[4,128,128]{2,1,0:T(8,128)(2,1)} fusion(bf16[4,128,256]{2,1,0:T(8,128)(2,1)} %get-tuple-element.7, bf16[4,256,128]{2,1,0:T(8,128)(2,1)} %bitcast.4), kind=kOutput, calls=%fused_computation | convolution fusion | flops 33619968 | bytes 655360 | tf_op jit(solution)/shard_map/tpk,tkc->tpc/dot_general | solution.py:194

commit v4 on v3

--- a/solution.py
+++ b/solution.py
@@ -167,11 +167,11 @@
     gathered, weights = pl.pallas_call(
         functools.partial(ladder_kernel, n_vir, n_occ, relays, by_tile),
         out_shape=(
-            jax.ShapeDtypeStruct((tiles, pair_dev, width), kind),
-            jax.ShapeDtypeStruct((choices, steps, depth, columns), kind),
+            pltpu.VMEM((tiles, pair_dev, width), kind),
+            pltpu.VMEM((choices, steps, depth, columns), kind),
         ),
         in_specs=[hbm] * 5,
-        out_specs=(hbm, hbm),
+        out_specs=(pl.BlockSpec(memory_space=pltpu.VMEM),) * 2,
         scratch_shapes=[
             pltpu.SMEM(pair_irrep.shape, jnp.int32),
             pltpu.SMEM(panel_blocks.shape, jnp.int32),

time: 20.7 us -> 19.6 us (0.947)
  matrix products: 1.9 us -> 0.87 us
    dot_general x1, matrix products: 1.9 us -> 0.87 us  [per_device(): jnp.einsum('tpk,tkc->tpc', gathered, weights, preferred_element_type=jnp....]
where the time goes in v4:
time: 19.6 us; the launch traced here: 19.5 us
  Pallas kernels  18.6 us (95%)
  matrix products  0.87 us (4%)
    pallas_call x1, Pallas kernels, per_device(): pl.pallas_call(functools.partial(ladder_kernel, n_vir, n_occ, relays, by_...  18.6 us
    dot_general x1, matrix products, per_device(): jnp.einsum('tpk,tkc->tpc', gathered, weights, preferred_element_type=jnp....  0.87 us

profile of v4, /device:TPU:0, one launch (start us, length us, event | category | flops | bytes accessed | tf_op | source)
XLA Modules:
  0.0 19.5 jit_solution(8460928560111655756)
XLA Ops:
  0.0 18.6 %shard_map.55 = (bf16[4,128,256]{2,1,0:T(8,128)(2,1)S(1)}, bf16[4,2,128,128]{3,2,1,0:T(8,128)(2,1)S(1)}) custom-call(s32[4]{0:T(128)} %labels_hbm.1, s32[1,8]{1,0:T(1,128)} %blocks_hbm.1, s32[2]{0:T(128)} %owner_hbm.1, bf16[128,256]{1,0:T(8,128)(2,1)} %amp_ref.1, bf16[1,8,128,128]{3,2,1,0:T(8,128)(2,1)} %panel_hbm.1), custom_call_target="tpu_custom_call" | custom-call | tf_op jit(solution)/shard_map/pallas_call | solution.py:167
  18.6 0.9 %convolution_convert_fusion = bf16[4,128,128]{2,1,0:T(8,128)(2,1)} fusion(bf16[4,128,256]{2,1,0:T(8,128)(2,1)S(1)} %get-tuple-element.7, bf16[4,256,128]{2,1,0:T(8,128)(2,1)S(1)} %bitcast.4), kind=kOutput, calls=%fused_computation | convolution fusion | flops 33619968 | bytes 655360 | tf_op jit(solution)/shard_map/tpk,tkc->tpc/dot_general | solution.py:194

commit v5 on v4

--- a/solution.py
+++ b/solution.py
@@ -32,6 +32,7 @@
     piece = stage.shape[2]
     full = relays == n_vir
     is_relay = vir < relays
+    both_ways = [d for near in range(1, n_vir // 2 + 1) for d in sorted({near, n_vir - near})]
 
     barrier = pltpu.get_barrier_semaphore()
     for d in range(1, n_vir):
@@ -102,11 +103,8 @@
     if by_tile:
         for d in range(1, n_vir):
             guarded(full, lax.rem(vir + d, n_vir) < relays, lambda d=d: info_copy(d).start())
-    for d in range(1, n_vir):
+    for d in both_ways:
         guarded(full, lax.rem(vir + d, n_vir) < relays, lambda d=d: one_copy(d).start())
-    for d in range(1, n_occ):
-        amp_copy(d).start()
-
     def relay():
         got[vir] = stage[vir]
         if by_tile:
@@ -118,7 +116,7 @@
         for d in range(1, n_vir):
             wait_one_from_stage(d)
         owners = [owner_ref[s] for s in range(steps)]
-        for d in list(range(1, n_vir)) + [0]:
+        for d in both_ways + [0]:
             to = lax.rem(vir + d, n_vir)
             if by_tile:
                 for t in range(tiles):
@@ -134,6 +132,8 @@
         own_rows().start()
 
     guarded(full, is_relay, relay)
+    for d in range(1, n_occ):
+        amp_copy(d).start()
 
     for d in range(1, n_occ):
         amp_copy(d).wait_recv()

time: 19.6 us -> 19.6 us (level)
  no operation moved by 1% of the time
where the time goes in v5:
time: 19.6 us; the launch traced here: 19.5 us
  Pallas kernels  18.6 us (95%)
  matrix products  0.87 us (4%)
    pallas_call x1, Pallas kernels, per_device(): pl.pallas_call(functools.partial(ladder_kernel, n_vir, n_occ, relays, by_...  18.6 us
    dot_general x1, matrix products, per_device(): jnp.einsum('tpk,tkc->tpc', gathered, weights, preferred_element_type=jnp....  0.87 us

profile of v5, /device:TPU:0, one launch (start us, length us, event | category | flops | bytes accessed | tf_op | source)
XLA Modules:
  0.0 19.5 jit_solution(17559226954283282602)
XLA Ops:
  0.0 18.6 %shard_map.55 = (bf16[4,128,256]{2,1,0:T(8,128)(2,1)S(1)}, bf16[4,2,128,128]{3,2,1,0:T(8,128)(2,1)S(1)}) custom-call(s32[4]{0:T(128)} %labels_hbm.1, s32[1,8]{1,0:T(1,128)} %blocks_hbm.1, s32[2]{0:T(128)} %owner_hbm.1, bf16[128,256]{1,0:T(8,128)(2,1)} %amp_ref.1, bf16[1,8,128,128]{3,2,1,0:T(8,128)(2,1)} %panel_hbm.1), custom_call_target="tpu_custom_call" | custom-call | tf_op jit(solution)/shard_map/pallas_call | solution.py:167
  18.6 0.9 %convolution_convert_fusion = bf16[4,128,128]{2,1,0:T(8,128)(2,1)} fusion(bf16[4,128,256]{2,1,0:T(8,128)(2,1)S(1)} %get-tuple-element.7, bf16[4,256,128]{2,1,0:T(8,128)(2,1)S(1)} %bitcast.4), kind=kOutput, calls=%fused_computation | convolution fusion | flops 33619968 | bytes 655360 | tf_op jit(solution)/shard_map/tpk,tkc->tpc/dot_general | solution.py:194

commit v6 on v5

--- a/solution.py
+++ b/solution.py
@@ -70,20 +70,20 @@
 
     def info_copy(d):
         return pltpu.make_async_remote_copy(
-            src_ref=info, dst_ref=info_all.at[vir], send_sem=info_send.at[d], recv_sem=info_recv.at[d],
+            src_ref=info, dst_ref=info_all.at[vir], send_sem=info_send.at[0 if full else d], recv_sem=info_recv.at[0 if full else d],
             device_id={"vir": lax.rem(vir + d, n_vir)}, device_id_type=MESH)
 
     def one_copy(d):
         to = lax.rem(vir + d, n_vir)
         return pltpu.make_async_remote_copy(
-            src_ref=stage.at[to], dst_ref=got.at[vir], send_sem=one_send.at[d], recv_sem=one_recv.at[d],
+            src_ref=stage.at[to], dst_ref=got.at[vir], send_sem=one_send.at[0 if full else d], recv_sem=one_recv.at[0 if full else d],
             device_id={"vir": to}, device_id_type=MESH)
 
     def two_copy(d):
         return pltpu.make_async_remote_copy(
             src_ref=picked.at[d if by_tile else 0],
             dst_ref=weights.at[:, :, pl.ds(pl.multiple_of(vir * piece, piece), piece), :],
-            send_sem=two_send.at[d], recv_sem=two_recv.at[d],
+            send_sem=two_send.at[0 if full else d], recv_sem=two_recv.at[0 if full else d],
             device_id={"vir": lax.rem(vir + d, n_vir)}, device_id_type=MESH)
 
     def own_rows():
@@ -97,8 +97,16 @@
 
     def wait_one_from_stage(d):
         pltpu.make_async_remote_copy(
-            src_ref=stage.at[0], dst_ref=got.at[vir], send_sem=one_send.at[d], recv_sem=one_recv.at[d],
+            src_ref=stage.at[0], dst_ref=got.at[vir], send_sem=one_send.at[0 if full else d], recv_sem=one_recv.at[0 if full else d],
             device_id={"vir": lax.rem(vir + d, n_vir)}, device_id_type=MESH).wait_recv()
+
+    def wait_all(semaphore, like):
+        pltpu.make_async_copy(like, like, semaphore.at[0]).wait()
+
+    others = n_vir - 1
+    all_info = info_all.at[pl.ds(0, others)]
+    all_one = got.at[pl.ds(0, others)]
+    all_two = weights.at[:, :, pl.ds(0, others * piece), :] if full else None
 
     if by_tile:
         for d in range(1, n_vir):
@@ -108,12 +116,16 @@
     def relay():
         got[vir] = stage[vir]
         if by_tile:
-            for d in range(1, n_vir):
+            if full:
+                wait_all(info_recv, all_info)
+            for d in range(1, 1 if full else n_vir):
                 info_copy(d).wait_recv()
             to_smem = pltpu.make_async_copy(info_all, info_smem, local_sem)
             to_smem.start()
             to_smem.wait()
-        for d in range(1, n_vir):
+        if full:
+            wait_all(one_recv, all_one)
+        for d in range(1, 1 if full else n_vir):
             wait_one_from_stage(d)
         owners = [owner_ref[s] for s in range(steps)]
         for d in both_ways + [0]:
@@ -137,14 +149,21 @@
 
     for d in range(1, n_occ):
         amp_copy(d).wait_recv()
-    for d in range(1, n_vir):
+    if full:
+        wait_all(two_recv, all_two)
+    for d in range(1, 1 if full else n_vir):
         guarded(full, lax.rem(vir + n_vir - d, n_vir) < relays, lambda d=d: two_copy(d).wait_recv())
 
     fetches[4].wait()
     guarded(full, is_relay, lambda: own_rows().wait())
     for d in range(1, n_occ):
         amp_copy(d).wait_send()
-    for d in range(1, n_vir):
+    if full:
+        if by_tile:
+            wait_all(info_send, all_info)
+        wait_all(one_send, all_one)
+        wait_all(two_send, all_two)
+    for d in range(1, 1 if full else n_vir):
         if by_tile:
             guarded(full, lax.rem(vir + d, n_vir) < relays, lambda d=d: info_copy(d).wait_send())
         guarded(full, lax.rem(vir + d, n_vir) < relays, lambda d=d: one_copy(d).wait_send())

time: 19.6 us -> 19.6 us (level)
  no operation moved by 1% of the time
where the time goes in v6:
time: 19.6 us; the launch traced here: 19.5 us
  Pallas kernels  18.6 us (95%)
  matrix products  0.87 us (4%)
    pallas_call x1, Pallas kernels, per_device(): pl.pallas_call(functools.partial(ladder_kernel, n_vir, n_occ, relays, by_...  18.6 us
    dot_general x1, matrix products, per_device(): jnp.einsum('tpk,tkc->tpc', gathered, weights, preferred_element_type=jnp....  0.87 us

profile of v6, /device:TPU:0, one launch (start us, length us, event | category | flops | bytes accessed | tf_op | source)
XLA Modules:
  0.0 19.5 jit_solution(10443839649403482610)
XLA Ops:
  0.0 18.6 %shard_map.55 = (bf16[4,128,256]{2,1,0:T(8,128)(2,1)S(1)}, bf16[4,2,128,128]{3,2,1,0:T(8,128)(2,1)S(1)}) custom-call(s32[4]{0:T(128)} %labels_hbm.1, s32[1,8]{1,0:T(1,128)} %blocks_hbm.1, s32[2]{0:T(128)} %owner_hbm.1, bf16[128,256]{1,0:T(8,128)(2,1)} %amp_ref.1, bf16[1,8,128,128]{3,2,1,0:T(8,128)(2,1)} %panel_hbm.1), custom_call_target="tpu_custom_call" | custom-call | tf_op jit(solution)/shard_map/pallas_call | solution.py:186
  18.6 0.9 %convolution_convert_fusion = bf16[4,128,128]{2,1,0:T(8,128)(2,1)} fusion(bf16[4,128,256]{2,1,0:T(8,128)(2,1)S(1)} %get-tuple-element.7, bf16[4,256,128]{2,1,0:T(8,128)(2,1)S(1)} %bitcast.4), kind=kOutput, calls=%fused_computation | convolution fusion | flops 33619968 | bytes 655360 | tf_op jit(solution)/shard_map/tpk,tkc->tpc/dot_general | solution.py:213
